TPU v7x, 32 devices: a whole 2x2x4 slice. The times are simulated.
32 devices in a mesh: rep: 4 (over y, x), fsdp: 8 (over z, core).
Axes of the slice: x: 2, y: 2, z: 4, core: 2. Of those that a mesh axis runs over, the one named last changes fastest.
Arguments:
- tokens: bfloat16 [16384, 8192], P(('rep', 'fsdp')), may hold values from -6 to 6
- norm_gain: bfloat16 [8192], replicated, may hold values from 0.5 to 1.5
- step_counts: int32 [4], P('rep'), may hold values from 25 to 100
- local_params: bfloat16 [4, 8192, 1024], P('rep', 'fsdp'), may hold values from -6 to 6
- global_params: float32 [8192, 1024], P('fsdp', 'rep'), may hold values from -6 to 6
- momentum: float32 [8192, 1024], P('fsdp', 'rep'), may hold values from -3 to 3
Outputs:
- keys_values: bfloat16 [16384, 1024], P(('rep', 'fsdp'))
- new_local: bfloat16 [4, 8192, 1024], P('rep', 'fsdp')
- new_global: float32 [8192, 1024], P('fsdp', 'rep')
- new_momentum: float32 [8192, 1024], P('fsdp', 'rep')
All inputs are finite; a program needn't handle non-finite values.
Results may differ from a plain program's by a relative error of at most 0.0057.
Values may be sent and summed in bfloat16 or wider, within the bound.
A program may use at most 128 MiB of HBM per device.

v0:
```python
import jax
import jax.numpy as jnp
from jax import lax
from jax.sharding import PartitionSpec as P


def nesterov(old_global, old_moment, average):
    delta = old_global - average
    moment_next = 0.9 * old_moment + delta
    global_next = old_global - 0.7 * (delta + 0.9 * moment_next)
    return (global_next, moment_next)


def shards(tokens, norm_gain, step_counts, local_params, global_params, momentum):
    counts = step_counts.astype(jnp.float32)
    total = lax.psum(jnp.sum(counts), "rep")
    mine = local_params[0].astype(jnp.float32)
    term = counts[0] * mine
    summed = lax.psum_scatter(term, "rep", scatter_dimension=1, tiled=True)
    new_global, new_momentum = nesterov(global_params, momentum, summed / total)
    full_global = lax.all_gather(new_global, "rep", axis=1, tiled=True)
    mixed = (0.5 * mine + 0.5 * full_global).astype(jnp.bfloat16)
    wide = tokens.astype(jnp.float32)
    square = jnp.mean(wide * wide, axis=1, keepdims=True)
    normed = (wide * lax.rsqrt(square + 1e-05) * norm_gain.astype(jnp.float32)).astype(jnp.bfloat16)
    product = jnp.dot(
        normed,
        lax.all_gather(mixed, "fsdp", axis=0, tiled=True),
        preferred_element_type=jnp.float32,
    )
    keys_values = (product * normed.shape[1] ** (-0.5)).astype(jnp.bfloat16)
    return (keys_values, mixed[None], new_global, new_momentum)


def solution(mesh):
    placed = (
        P(("rep", "fsdp"), None),
        P(),
        P("rep"),
        P("rep", "fsdp", None),
        P("fsdp", "rep"),
        P("fsdp", "rep"),
    )
    return jax.shard_map(
        shards,
        mesh=mesh,
        in_specs=placed,
        out_specs=(
            P(("rep", "fsdp"), None),
            P("rep", "fsdp", None),
            P("fsdp", "rep"),
            P("fsdp", "rep"),
        ),
        check_vma=False,
    )
```

profile of v0, /device:TPU:0, one launch (start us, length us, event | category | flops | bytes accessed | tf_op | source)
XLA Modules:
  0.0 301.9 jit_solution(15414504060828957148)
XLA Ops:
  7.2 0.0 reduce-scatter.2.cloned.1.call-start
  7.9 0.0 copy-start.1
  7.9 4.2 %convert_multiply_fusion.2 = f32[1024,1024]{1,0:T(8,128)} fusion(bf16[1,1024,1024]{2,1,0:T(8,128)(2,1)} %param.9, f32[]{:T(128)} %bitcast.1), kind=kLoop, calls=%fused_computation.9 | loop fusion | flops 2097152 | bytes 6291460 | tf_op jit(solution)/shard_map/mul | solution.py:18
  12.1 0.0 reduce-scatter.2.cloned.1.call-update
  12.1 0.0 copy-start
  12.1 0.0 all-gather.3.cloned.1.call-start
  12.2 12.6 %psum.7 = f32[]{:T(128)} all-reduce(f32[]{:T(128)} %bitcast.1), channel_id=1, replica_groups=mesh['rep'=4,'fsdp'=8] {'rep'}, use_global_device_ids=true, to_apply=%region_2.0 | all-reduce | flops 1 | bytes 8 | tf_op jit(solution)/shard_map/psum | solution.py:16
  24.7 42.9 %reduce-scatter.2.cloned.1.call-done = f32[1024,256]{1,0:T(8,128)} async-done(((f32[1024,1024]{1,0:T(8,128)}), f32[1024,256]{1,0:T(8,128)}) %reduce-scatter.2.cloned.1.call-update) | async-done | bytes 1048592 | tf_op jit(solution)/shard_map/reduce_scatter | solution.py:19
  67.6 0.0 copy-done.1
  67.6 3.8 %multiply_subtract_fusion = (f32[1024,256]{1,0:T(8,128)}, f32[1024,256]{1,0:T(8,128)}) fusion(f32[1024,256]{1,0:T(8,128)S(1)} %copy-done.1, f32[1024,256]{1,0:T(8,128)} %reduce-scatter.2.cloned.1.call-done, f32[]{:T(128)} %psum.7, f32[1024,256]{1,0:T(8,128)} %param.11), kind=kLoop, calls=%fused_computation.13 | loop fusion | flops 2097152 | bytes 5242884 | tf_op jit(solution)/shard_map/sub | solution.py:10
  71.4 0.0 all-gather.3.cloned.1.call-update
  71.4 0.0 copy-start.2
  71.4 0.0 all-gather.5.cloned.1.call-start
  71.5 52.6 %all-gather.3.cloned.1.call-done = f32[1024,1024]{1,0:T(8,128)} async-done(((f32[1024,256]{1,0:T(8,128)}), f32[1024,1024]{1,0:T(8,128)}) %all-gather.3.cloned.1.call-update) | async-done | bytes 4194320 | tf_op jit(solution)/shard_map/all_gather | solution.py:21
  124.1 0.0 copy-done
  124.1 4.3 %fusion.8 = bf16[1024,1024]{1,0:T(8,128)(2,1)} fusion(f32[1024,1024]{1,0:T(8,128)} %all-gather.3.cloned.1.call-done, bf16[1,1024,1024]{2,1,0:T(8,128)(2,1)S(1)} %copy-done), kind=kLoop, calls=%fused_computation.11 | loop fusion | flops 4194304 | bytes 8388608 | tf_op jit(solution)/shard_map/convert_element_type | solution.py:22
  128.4 0.0 all-gather.5.cloned.1.call-update
  128.4 0.0 copy-done.2
  128.5 5.1 %fusion = f32[512]{0:T(512)S(1)} fusion(bf16[512,8192]{1,0:T(8,128)(2,1)} %param.6), kind=kLoop, calls=%fused_computation.2 | loop fusion | flops 12582400 | bytes 8390656 | tf_op jit(solution)/shard_map/reduce_sum | solution.py:24
  133.6 146.1 %all-gather.5.cloned.1.call-done = bf16[8192,1024]{1,0:T(8,128)(2,1)} async-done(((bf16[1024,1024]{1,0:T(8,128)(2,1)}), bf16[8192,1024]{1,0:T(8,128)(2,1)}) %all-gather.5.cloned.1.call-update) | async-done | bytes 16777232 | tf_op jit(solution)/shard_map/all_gather | solution.py:28
  279.7 15.7 %multiply_convert_fusion = bf16[512,1024]{1,0:T(8,128)(2,1)} fusion(bf16[8192,1024]{1,0:T(8,128)(2,1)} %all-gather.5.cloned.1.call-done, bf16[512,8192]{1,0:T(8,128)(2,1)} %param.6, f32[8192]{0:T(1024)S(1)} %convert_element_type.25, f32[512]{0:T(512)S(1)} %add_rsqrt_fusion), kind=kOutput, calls=%fused_computation.12 | convolution fusion | flops 8607760384 | bytes 26249216 | tf_op jit(solution)/shard_map/dot_general | solution.py:26
  (2 shorter events, 0.0 us)
Async XLA Ops:
  7.2 60.5 %reduce-scatter.2.cloned.1.call-start = ((), (), s32[]{:S(2)}) async-start(), calls=%async_computation.1 | async-start | bytes 5242880 | tf_op jit(solution)/shard_map/reduce_scatter | solution.py:19
  7.9 59.8 %copy-start.1 = (f32[1024,256]{1,0:T(8,128)S(1)}, f32[1024,256]{1,0:T(8,128)}, u32[]{:S(2)}) copy-start(f32[1024,256]{1,0:T(8,128)} %param.10) | copy-start | bytes 3145732
  12.1 112.0 %copy-start = (bf16[1,1024,1024]{2,1,0:T(8,128)(2,1)S(1)}, bf16[1,1024,1024]{2,1,0:T(8,128)(2,1)}, u32[]{:S(2)}) copy-start(bf16[1,1024,1024]{2,1,0:T(8,128)(2,1)} %param.9) | copy-start | bytes 6291460
  12.1 112.0 %all-gather.3.cloned.1.call-start = ((), (), s32[]{:S(2)}) async-start(), calls=%async_computation.2 | async-start | bytes 5242880 | tf_op jit(solution)/shard_map/all_gather | solution.py:21
  71.4 57.0 %copy-start.2 = (bf16[8192]{0:T(1024)(128)(2,1)S(1)}, bf16[8192]{0:T(1024)(128)(2,1)}, u32[]{:S(2)}) copy-start(bf16[8192]{0:T(1024)(128)(2,1)} %param.7) | copy-start | bytes 49156
  71.4 208.3 %all-gather.5.cloned.1.call-start = ((), (), s32[]{:S(2)}) async-start(), calls=%async_computation.3 | async-start | bytes 18874368 | tf_op jit(solution)/shard_map/all_gather | solution.py:28
Sparse Core Ops, SparseCore 0:
  12.2 55.3 reduce-scatter.1
  71.6 52.5 all-gather.2
  128.6 151.1 all-gather.4
where the time goes:
time: 302 us
  waiting for transfers between devices  242 us (80%)
  other arithmetic  17.4 us (6%)
  matrix products  15.7 us (5%)
  between operations  14.4 us (5%)
  blocking collectives  12.6 us (4%)
    all_gather x1, waiting for transfers between devices, shards(): lax.all_gather(mixed, 'fsdp', axis=0, tiled=True)  146 us
    all_gather x1, waiting for transfers between devices, shards(): full_global = lax.all_gather(new_global, 'rep', axis=1, tiled=True)  52.6 us
    reduce_scatter x1, waiting for transfers between devices, shards(): summed = lax.psum_scatter(term, 'rep', scatter_dimension=1, tiled=True)  42.9 us
    dot_general x1, matrix products, shards(): jnp.dot(normed, lax.all_gather(mixed, 'fsdp', axis=0, tiled=True), prefer...  15.7 us
    psum x1, blocking collectives, shards(): total = lax.psum(jnp.sum(counts), 'rep')  12.6 us
  transfers between devices with their start and end apart: 3, of which 3 were waited for; matrix products, arithmetic and copies ran while one was open for 2% of the time, Pallas kernels for 0%

commit v1 on v0

v1 whole, which is shorter than its diff:
```python
import functools

import jax
import jax.numpy as jnp
from jax import lax
from jax.experimental import pallas as pl
from jax.experimental.pallas import tpu as pltpu
from jax.sharding import PartitionSpec as P

MESH = pl.DeviceIdType.MESH
BF16 = jnp.bfloat16
F32 = jnp.float32


def kernel(
    n_rep, n_line, chunk, step,
    counts, gain, tok_hbm, loc_hbm, glob_hbm, mom_hbm,
    kv_out, nl_out, ng_out, nm_out,
    tok, w, loc, glob, mom, got, ag, cnt, acc, kv,
    load_sem, out_sem, cs, cr, rss, rsr, ags, agr, zr, zu, zd, ss, sr,
):
    me = lax.axis_index("rep")
    f = lax.axis_index("fsdp")
    z = f // 2
    core = f % 2
    rows, cols = loc.shape
    part = cols // n_rep
    n_chunk = rows // chunk

    def load(i, src, dst):
        return pltpu.make_async_copy(src, dst, load_sem.at[i])

    loads = [
        load(0, loc_hbm.at[0], loc),
        load(1, glob_hbm, glob),
        load(2, mom_hbm, mom),
        load(3, tok_hbm, tok),
    ]
    for one in loads:
        one.start()
    cnt[me] = jnp.full(cnt.shape[1:], counts[0].astype(F32), F32)

    barrier = pltpu.get_barrier_semaphore()
    for j in range(1, n_rep):
        pl.semaphore_signal(barrier, inc=1, device_id={"rep": (me + j) % n_rep}, device_id_type=MESH)
    pl.semaphore_signal(barrier, inc=1, device_id={"fsdp": z * 2 + 1 - core}, device_id_type=MESH)

    @pl.when(z > 0)
    def _():
        pl.semaphore_signal(barrier, inc=1, device_id={"fsdp": f - 2}, device_id_type=MESH)

    @pl.when(z < n_line - 1)
    def _():
        pl.semaphore_signal(barrier, inc=1, device_id={"fsdp": f + 2}, device_id_type=MESH)

    ends = (z == 0).astype(jnp.int32) + (z == n_line - 1).astype(jnp.int32)
    pl.semaphore_wait(barrier, n_rep + 2 - ends)

    def span(k):
        return pl.ds(pl.multiple_of(k * chunk, chunk), chunk)

    def slot(p):
        return pl.ds(pl.multiple_of(p * part, part), part)

    def count_copy(j, owner):
        return pltpu.make_async_remote_copy(
            cnt.at[owner], cnt.at[owner], cs.at[j - 1], cr.at[j - 1],
            device_id={"rep": (me + j) % n_rep}, device_id_type=MESH)

    def part_copy(j, k):
        to = (me + j) % n_rep
        return pltpu.make_async_remote_copy(
            loc.at[span(k), slot(to)], got.at[me, span(k)], rss.at[j - 1, k], rsr.at[j - 1, k],
            device_id={"rep": to}, device_id_type=MESH)

    def part_wait(j, k):
        owner = (me + n_rep - j) % n_rep
        pltpu.make_async_remote_copy(
            got.at[owner, span(k)], got.at[owner, span(k)], rss.at[j - 1, k], rsr.at[j - 1, k],
            device_id={"rep": (me + j) % n_rep}, device_id_type=MESH).wait_recv()

    def new_copy(j, k, owner):
        return pltpu.make_async_remote_copy(
            ag.at[owner, span(k)], ag.at[owner, span(k)], ags.at[j - 1, k], agr.at[j - 1, k],
            device_id={"rep": (me + j) % n_rep}, device_id_type=MESH)

    def line_copy(src, k, up):
        sem = zu if up else zd
        block = w.at[src * 2 + core, span(k)]
        return pltpu.make_async_remote_copy(
            block, block, sem.at[src, k], zr.at[src, k],
            device_id={"fsdp": f + 2 if up else f - 2}, device_id_type=MESH)

    def pair_copy(src, k, owner):
        block = w.at[src * 2 + owner, span(k)]
        return pltpu.make_async_remote_copy(
            block, block, ss.at[src, k], sr.at[src, k],
            device_id={"fsdp": z * 2 + 1 - core}, device_id_type=MESH)

    def send_parts(k):
        for j in range(1, n_rep):
            part_copy(j, k).start()

    def pass_on(src, k, up, down):
        @pl.when(jnp.logical_and(up, z < n_line - 1))
        def _():
            line_copy(src, k, True).start()

        @pl.when(jnp.logical_and(down, z > 0))
        def _():
            line_copy(src, k, False).start()

        pair_copy(src, k, core).start()

    loads[0].wait()
    for j in range(1, n_rep):
        count_copy(j, me).start()
    ahead = min(2, n_chunk)
    for k in range(ahead):
        send_parts(k)
    loads[1].wait()
    loads[2].wait()
    for j in range(1, n_rep):
        count_copy(j, (me + n_rep - j) % n_rep).wait_recv()
    total = cnt[0, 0:1, :]
    for r in range(1, n_rep):
        total = total + cnt[r, 0:1, :]

    def reduce_chunk(k):
        for j in range(1, n_rep):
            part_wait(j, k)

        def some(i, carry):
            at = pl.ds(pl.multiple_of(k * chunk + i * step, step), step)
            summed = cnt[me, 0:1, :] * loc[at, slot(me)].astype(F32)
            for j in range(1, n_rep):
                r = (me + j) % n_rep
                summed = summed + cnt[r, 0:1, :] * got[r, at, :].astype(F32)
            old = glob[at, :]
            delta = old - summed / total
            moment = 0.9 * mom[at, :] + delta
            new = old - 0.7 * (delta + 0.9 * moment)
            mom[at, :] = moment
            glob[at, :] = new
            ag[me, at, :] = new.astype(BF16)
            return carry

        lax.fori_loop(0, chunk // step, some, 0)
        for j in range(1, n_rep):
            new_copy(j, k, me).start()

    def mix_chunk(k):
        for j in range(1, n_rep):
            new_copy(j, k, (me + n_rep - j) % n_rep).wait_recv()

        def some(i, carry):
            at = pl.ds(pl.multiple_of(k * chunk + i * step, step), step)
            for r in range(n_rep):
                c = slice(r * part, (r + 1) * part)
                mixed = 0.5 * loc[at, c].astype(F32) + 0.5 * ag[r, at, :].astype(F32)
                w[f, at, c] = mixed.astype(BF16)
            return carry

        lax.fori_loop(0, chunk // step, some, 0)
        pass_on(z, k, True, True)

    def norm():
        loads[3].wait()

        def some(i, carry):
            at = pl.ds(pl.multiple_of(i * 16, 16), 16)
            wide = tok[at, :].astype(F32)
            square = jnp.mean(wide * wide, axis=1, keepdims=True)
            tok[at, :] = (wide * lax.rsqrt(square + 1e-05) * gain[...].astype(F32)).astype(BF16)
            return carry

        lax.fori_loop(0, tok.shape[0] // 16, some, 0)
        acc[...] = jnp.zeros_like(acc)

    for k in range(n_chunk):
        reduce_chunk(k)
        if k + ahead < n_chunk:
            send_parts(k + ahead)
        if k >= 1:
            mix_chunk(k - 1)
        if k == min(1, n_chunk - 1):
            norm()
    mix_chunk(n_chunk - 1)

    outs = [
        pltpu.make_async_copy(glob, ng_out, out_sem.at[0]),
        pltpu.make_async_copy(mom, nm_out, out_sem.at[1]),
        pltpu.make_async_copy(w.at[f], nl_out.at[0], out_sem.at[2]),
    ]
    for one in outs:
        one.start()

    wide_cols = min(256, cols)

    def multiply(at, k):
        a = tok[:, pl.ds(pl.multiple_of(at * rows + k * chunk, chunk), chunk)]

        def some(i, carry):
            c = pl.ds(pl.multiple_of(i * wide_cols, wide_cols), wide_cols)
            acc[:, c] += jnp.dot(a, w[at, span(k), c], preferred_element_type=F32)
            return carry

        lax.fori_loop(0, cols // wide_cols, some, 0)

    def compute(src, k):
        multiply(src * 2 + core, k)
        pair_copy(src, k, 1 - core).wait_recv()
        multiply(src * 2 + 1 - core, k)

    def own(k, carry):
        compute(z, k)
        return carry

    def receive(t):
        d = t // n_chunk
        k = t % n_chunk

        @pl.when(z - d >= 0)
        def _():
            line_copy(z - d, k, True).wait_recv()
            pass_on(z - d, k, True, False)

        @pl.when(z + d < n_line)
        def _():
            line_copy(z + d, k, False).wait_recv()
            pass_on(z + d, k, False, True)

    def finish(t):
        d = t // n_chunk
        k = t % n_chunk

        @pl.when(z - d >= 0)
        def _():
            compute(z - d, k)

        @pl.when(jnp.logical_and(z + d < n_line, d > 0))
        def _():
            compute(z + d, k)

    def event(t, carry):
        receive(t)
        finish(t - n_chunk)
        return carry

    n_event = n_line * n_chunk
    lag = 1
    for t in range(min(lag, n_event - n_chunk)):
        receive(n_chunk + t)
    lax.fori_loop(0, n_chunk, own, 0)

    def later(t, carry):
        receive(t)
        finish(t - lag)
        return carry

    lax.fori_loop(n_chunk + lag, n_event, later, 0)
    for t in range(n_event - lag, n_event):
        finish(t)

    scale = (n_line * 2 * rows) ** (-0.5)

    def scaled(i, carry):
        at = pl.ds(pl.multiple_of(i * 64, 64), 64)
        kv[at, :] = (acc[at, :] * scale).astype(BF16)
        return carry

    lax.fori_loop(0, acc.shape[0] // 64, scaled, 0)
    last = pltpu.make_async_copy(kv, kv_out, out_sem.at[3])
    last.start()

    for j in range(1, n_rep):
        count_copy(j, me).wait_send()

    def sent(k, carry):
        for j in range(1, n_rep):
            part_copy(j, k).wait_send()
            new_copy(j, k, me).wait_send()
        return carry

    lax.fori_loop(0, n_chunk, sent, 0)

    def passed(t, carry):
        src = t // n_chunk
        k = t % n_chunk

        @pl.when(jnp.logical_and(src <= z, z < n_line - 1))
        def _():
            line_copy(src, k, True).wait_send()

        @pl.when(jnp.logical_and(src >= z, z > 0))
        def _():
            line_copy(src, k, False).wait_send()

        pair_copy(src, k, core).wait_send()
        return carry

    lax.fori_loop(0, n_event, passed, 0)
    for one in outs:
        one.wait()
    last.wait()


def shards(n_rep, n_fsdp, tokens, norm_gain, step_counts, local_params, global_params, momentum):
    count, width = tokens.shape
    _, rows, cols = local_params.shape
    part = cols // n_rep
    n_line = n_fsdp // 2
    chunk = min(128, rows)
    n_chunk = rows // chunk
    anywhere = pl.BlockSpec(memory_space=pl.ANY)
    dma = pltpu.SemaphoreType.DMA
    return pl.pallas_call(
        functools.partial(kernel, n_rep, n_line, chunk, 32),
        out_shape=(
            jax.ShapeDtypeStruct((count, cols), BF16),
            jax.ShapeDtypeStruct((1, rows, cols), BF16),
            jax.ShapeDtypeStruct((rows, part), F32),
            jax.ShapeDtypeStruct((rows, part), F32),
        ),
        in_specs=[
            pl.BlockSpec(memory_space=pltpu.SMEM),
            pl.BlockSpec(memory_space=pltpu.VMEM),
            anywhere, anywhere, anywhere, anywhere,
        ],
        out_specs=(anywhere,) * 4,
        scratch_shapes=[
            pltpu.VMEM((count, width), BF16),
            pltpu.VMEM((n_fsdp, rows, cols), BF16),
            pltpu.VMEM((rows, cols), BF16),
            pltpu.VMEM((rows, part), F32),
            pltpu.VMEM((rows, part), F32),
            pltpu.VMEM((n_rep, rows, part), BF16),
            pltpu.VMEM((n_rep, rows, part), BF16),
            pltpu.VMEM((n_rep, 8, part), F32),
            pltpu.VMEM((count, cols), F32),
            pltpu.VMEM((count, cols), BF16),
            dma((4,)), dma((4,)),
            dma((n_rep - 1,)), dma((n_rep - 1,)),
            dma((n_rep - 1, n_chunk)), dma((n_rep - 1, n_chunk)),
            dma((n_rep - 1, n_chunk)), dma((n_rep - 1, n_chunk)),
            dma((n_line, n_chunk)), dma((n_line, n_chunk)), dma((n_line, n_chunk)),
            dma((n_line, n_chunk)), dma((n_line, n_chunk)),
        ],
        compiler_params=pltpu.CompilerParams(
            collective_id=0, has_side_effects=True, vmem_limit_bytes=56 * 2**20
        ),
    )(step_counts, norm_gain.reshape(1, width), tokens, local_params, global_params, momentum)


def solution(mesh):
    return jax.shard_map(
        functools.partial(shards, mesh.shape["rep"], mesh.shape["fsdp"]),
        mesh=mesh,
        in_specs=(
            P(("rep", "fsdp"), None),
            P(),
            P("rep"),
            P("rep", "fsdp", None),
            P("fsdp", "rep"),
            P("fsdp", "rep"),
        ),
        out_specs=(
            P(("rep", "fsdp"), None),
            P("rep", "fsdp", None),
            P("fsdp", "rep"),
            P("fsdp", "rep"),
        ),
        check_vma=False,
    )
```

time: 302 us -> 171 us (0.57)
  waiting for transfers between devices: 242 us -> 0 us
  Pallas kernels: 0 us -> 161 us
  other arithmetic: 17.4 us -> 0 us
  matrix products: 15.7 us -> 0 us
  between operations: 14.4 us -> 1.3 us
  blocking collectives: 12.6 us -> 0 us
  local copies, waits for them, and re-layouts: 0.02 us -> 8.3 us
    all_gather x2 -> x0, waiting for transfers between devices: 199 us -> none  [the longest x1 146 us: shards(): lax.all_gather(mixed, 'fsdp', axis=0, tiled=True)]
    pallas_call x0 -> x1, Pallas kernels: none -> 161 us  [shards(): pl.pallas_call(functools.partial(kernel, n_rep, n_line, chunk, 32), out_s...]
    reduce_scatter x1 -> x0, waiting for transfers between devices: 42.9 us -> none  [shards(): summed = lax.psum_scatter(term, 'rep', scatter_dimension=1, tiled=True)]
    dot_general x1 -> x0, matrix products: 15.7 us -> none  [shards(): jnp.dot(normed, lax.all_gather(mixed, 'fsdp', axis=0, tiled=True), prefer...]
    psum x1 -> x0, blocking collectives: 12.6 us -> none  [shards(): total = lax.psum(jnp.sum(counts), 'rep')]
    unnamed x6 -> x10, local copies, waits for them, and re-layouts: 0.02 us -> 6.95 us
    reduce_sum x1 -> x0, other arithmetic: 5.1 us -> none  [shards(): square = jnp.mean(wide * wide, axis=1, keepdims=True)]
    convert_element_type x2 -> x0, other arithmetic: 4.29 us -> none  [the longest x1 4.28 us: shards(): mixed = (0.5 * mine + 0.5 * full_global).astype(jnp.bfloat16)]
  transfers between devices with their start and end apart: 3 -> 0, of which waited for: 3 -> 0; matrix products, arithmetic and copies ran while one was open for 2% -> 0% of each run, Pallas kernels for 0% -> 0%
where the time goes in v1:
time: 171 us; the launch traced here: 170 us
  Pallas kernels  161 us (94%)
  local copies, waits for them, and re-layouts  8.3 us (5%)
    pallas_call x1, Pallas kernels, shards(): pl.pallas_call(functools.partial(kernel, n_rep, n_line, chunk, 32), out_s...  161 us
    unnamed x10, local copies, waits for them, and re-layouts  6.95 us

profile of v1, /device:TPU:0, one launch (start us, length us, event | category | flops | bytes accessed | tf_op | source)
XLA Modules:
  0.0 170.4 jit_solution(11086078504671438025)
XLA Ops:
  1.3 1.4 reshape.11.gain
  2.6 160.8 %shard_map.93 = (bf16[512,1024]{1,0:T(8,128)(2,1)}, bf16[1,1024,1024]{2,1,0:T(8,128)(2,1)}, f32[1024,256]{1,0:T(8,128)}, f32[1024,256]{1,0:T(8,128)}) custom-call(s32[1]{0:T(128)S(6)} %copy.14.counts, bf16[1,8192]{1,0:T(2,128)(2,1)} %reshape.11.gain, bf16[512,8192]{1,0:T(8,128)(2,1)} %tok_hbm.1, bf16[1,1024,1024]{2,1,0:T(8,128)(2,1)} %loc_hbm.1, ...), custom_call_target="tpu_custom_call" | custom-call | tf_op jit(solution)/shard_map/pallas_call | solution.py:317
  163.4 0.0 copy-start
  163.4 2.4 %copy.15 = bf16[512,1024]{1,0:T(8,128)(2,1)} copy(bf16[512,1024]{1,0:T(8,128)(2,1)} %get-tuple-element.8) | data formatting | bytes 2097152
  165.8 0.0 copy-done
  165.8 0.0 copy-start.2
  165.8 1.3 copy.16
  167.1 0.6 copy-done.2
  167.8 0.0 copy-start.1
  167.8 1.0 copy.17
  168.8 0.6 copy-done.1
  169.4 1.0 copy.18
Async XLA Ops:
  163.4 2.4 %copy-start = (bf16[1,1024,1024]{2,1,0:T(8,128)(2,1)S(1)}, bf16[1,1024,1024]{2,1,0:T(8,128)(2,1)}, u32[]{:S(2)}) copy-start(bf16[1,1024,1024]{2,1,0:T(8,128)(2,1)} %get-tuple-element.9) | copy-start | bytes 6291460
  165.8 2.0 %copy-start.2 = (f32[1024,256]{1,0:T(8,128)S(1)}, f32[1024,256]{1,0:T(8,128)}, u32[]{:S(2)}) copy-start(f32[1024,256]{1,0:T(8,128)} %get-tuple-element.10) | copy-start | bytes 3145732
  167.8 1.6 copy-start.1

commit v2 on v1

--- a/solution.py
+++ b/solution.py
@@ -13,11 +13,11 @@
 
 
 def kernel(
-    n_rep, n_line, chunk, step,
+    n_rep, n_line, chunk, step, first,
     counts, gain, tok_hbm, loc_hbm, glob_hbm, mom_hbm,
     kv_out, nl_out, ng_out, nm_out,
-    tok, w, loc, glob, mom, got, ag, cnt, acc, kv,
-    load_sem, out_sem, cs, cr, rss, rsr, ags, agr, zr, zu, zd, ss, sr,
+    tok, w, loc, glob, mom, got, ag, cnt, acc, kv, lent, part_out, part_in,
+    load_sem, out_sem, cs, cr, rss, rsr, ags, agr, zr, zu, zd, ss, sr, ts, tr, ps, pr,
 ):
     me = lax.axis_index("rep")
     f = lax.axis_index("fsdp")
@@ -26,6 +26,26 @@
     rows, cols = loc.shape
     part = cols // n_rep
     n_chunk = rows // chunk
+    at_end = jnp.logical_or(z == 0, z == n_line - 1)
+    helps = jnp.logical_or(z == 1, z == n_line - 2)
+    low = z < n_line // 2
+    inward = jnp.where(low, f + 2, f - 2)
+    outward = jnp.where(low, f - 2, f + 2)
+    lend = first < n_chunk
+
+    def lent_out(dest, src, k):
+        if not lend:
+            return dest < 0
+        dist = jnp.where(dest == 0, src, n_line - 1 - src)
+        near = jnp.logical_or(dist == 1, dist == 2)
+        end = jnp.logical_or(dest == 0, dest == n_line - 1)
+        return jnp.logical_and(jnp.logical_and(end, near), k >= first)
+
+    def goes_up(src, k):
+        return jnp.logical_and(z < n_line - 1, jnp.logical_not(lent_out(z + 1, src, k)))
+
+    def goes_down(src, k):
+        return jnp.logical_and(z > 0, jnp.logical_not(lent_out(z - 1, src, k)))
 
     def load(i, src, dst):
         return pltpu.make_async_copy(src, dst, load_sem.at[i])
@@ -102,15 +122,48 @@
             part_copy(j, k).start()
 
     def pass_on(src, k, up, down):
-        @pl.when(jnp.logical_and(up, z < n_line - 1))
+        @pl.when(jnp.logical_and(up, goes_up(src, k)))
         def _():
             line_copy(src, k, True).start()
 
-        @pl.when(jnp.logical_and(down, z > 0))
+        @pl.when(jnp.logical_and(down, goes_down(src, k)))
         def _():
             line_copy(src, k, False).start()
 
         pair_copy(src, k, core).start()
+
+    def lent_block(q, low_end):
+        d = q // 2 + 1
+        return jnp.where(low_end, d, n_line - 1 - d) * 2 + q % 2
+
+    lent_rows = rows - first * chunk
+
+    def lent_copy(q):
+        at = pl.multiple_of(lent_block(q, low) * rows + first * chunk, chunk)
+        return pltpu.make_async_remote_copy(
+            tok.at[:, pl.ds(at, lent_rows)], lent.at[q], ts.at[q], tr.at[q],
+            device_id={"fsdp": inward}, device_id_type=MESH)
+
+    wide_cols = min(256, cols)
+    n_wide = cols // wide_cols
+
+    def part_back(i):
+        c = slice(i * wide_cols, (i + 1) * wide_cols)
+        return pltpu.make_async_remote_copy(
+            part_out.at[:, c], part_in.at[:, c], ps.at[i], pr.at[i],
+            device_id={"fsdp": outward}, device_id_type=MESH)
+
+    def help_end():
+        for q in range(4):
+            lent_copy(q).wait_recv()
+        for i in range(n_wide):
+            c = slice(i * wide_cols, (i + 1) * wide_cols)
+            summed = jnp.zeros((tok.shape[0], wide_cols), F32)
+            for q in range(4):
+                summed = summed + jnp.dot(
+                    lent[q], w[lent_block(q, low), first * chunk :, c], preferred_element_type=F32)
+            part_out[:, c] = summed.astype(BF16)
+            part_back(i).start()
 
     loads[0].wait()
     for j in range(1, n_rep):
@@ -162,7 +215,8 @@
             return carry
 
         lax.fori_loop(0, chunk // step, some, 0)
-        pass_on(z, k, True, True)
+        inner = jnp.logical_not(at_end) if lend else True
+        pass_on(z, k, inner, inner)
 
     def norm():
         loads[3].wait()
@@ -177,15 +231,42 @@
         lax.fori_loop(0, tok.shape[0] // 16, some, 0)
         acc[...] = jnp.zeros_like(acc)
 
+    if lend:
+        @pl.when(at_end)
+        def _():
+            norm()
+            for q in range(4):
+                lent_copy(q).start()
+
     for k in range(n_chunk):
         reduce_chunk(k)
         if k + ahead < n_chunk:
             send_parts(k + ahead)
         if k >= 1:
             mix_chunk(k - 1)
-        if k == min(1, n_chunk - 1):
+    mix_chunk(n_chunk - 1)
+
+    if lend:
+        @pl.when(at_end)
+        def _():
+            for q in range(4):
+                lent_copy(q).wait_send()
+
+        @pl.when(z == 0)
+        def _():
+            for k in range(n_chunk):
+                line_copy(z, k, True).start()
+
+        @pl.when(z == n_line - 1)
+        def _():
+            for k in range(n_chunk):
+                line_copy(z, k, False).start()
+
+        @pl.when(jnp.logical_not(at_end))
+        def _():
             norm()
-    mix_chunk(n_chunk - 1)
+    else:
+        norm()
 
     outs = [
         pltpu.make_async_copy(glob, ng_out, out_sem.at[0]),
@@ -195,8 +276,6 @@
     for one in outs:
         one.start()
 
-    wide_cols = min(256, cols)
-
     def multiply(at, k):
         a = tok[:, pl.ds(pl.multiple_of(at * rows + k * chunk, chunk), chunk)]
 
@@ -216,51 +295,50 @@
         compute(z, k)
         return carry
 
+    base = n_chunk * jnp.maximum(jnp.maximum(z - 1, n_line - 2 - z), 0)
+
+    def arrival(t, up):
+        room = z if up else n_line - 1 - z
+        early = t < base
+        k = jnp.where(early, t % n_chunk, t - base - room)
+        dist = jnp.where(early, t // n_chunk + 1, room)
+        src = z - dist if up else z + dist
+        inside = jnp.where(early, dist < room, room > 0)
+        there = jnp.logical_and(inside, jnp.logical_and(k >= 0, k < n_chunk))
+        return jnp.logical_and(there, jnp.logical_not(lent_out(z, src, k))), src, k
+
     def receive(t):
-        d = t // n_chunk
-        k = t % n_chunk
-
-        @pl.when(z - d >= 0)
-        def _():
-            line_copy(z - d, k, True).wait_recv()
-            pass_on(z - d, k, True, False)
-
-        @pl.when(z + d < n_line)
-        def _():
-            line_copy(z + d, k, False).wait_recv()
-            pass_on(z + d, k, False, True)
+        for up in (True, False):
+            there, src, k = arrival(t, up)
+
+            @pl.when(there)
+            def _():
+                line_copy(src, k, up).wait_recv()
+                pass_on(src, k, up, not up)
 
     def finish(t):
-        d = t // n_chunk
-        k = t % n_chunk
-
-        @pl.when(z - d >= 0)
-        def _():
-            compute(z - d, k)
-
-        @pl.when(jnp.logical_and(z + d < n_line, d > 0))
-        def _():
-            compute(z + d, k)
-
-    def event(t, carry):
-        receive(t)
-        finish(t - n_chunk)
-        return carry
+        for up in (True, False):
+            there, src, k = arrival(t, up)
+
+            @pl.when(there)
+            def _():
+                compute(src, k)
 
     n_event = n_line * n_chunk
-    lag = 1
-    for t in range(min(lag, n_event - n_chunk)):
-        receive(n_chunk + t)
+    n_tick = (n_line - 2) * n_chunk + n_chunk + n_line
+    receive(0)
     lax.fori_loop(0, n_chunk, own, 0)
 
     def later(t, carry):
         receive(t)
-        finish(t - lag)
+        finish(t - 1)
+        if lend:
+            @pl.when(jnp.logical_and(helps, t == base))
+            def _():
+                help_end()
         return carry
 
-    lax.fori_loop(n_chunk + lag, n_event, later, 0)
-    for t in range(n_event - lag, n_event):
-        finish(t)
+    lax.fori_loop(1, n_tick + 1, later, 0)
 
     scale = (n_line * 2 * rows) ** (-0.5)
 
@@ -268,6 +346,24 @@
         at = pl.ds(pl.multiple_of(i * 64, 64), 64)
         kv[at, :] = (acc[at, :] * scale).astype(BF16)
         return carry
+
+    if lend:
+        @pl.when(at_end)
+        def _():
+            for i in range(n_wide):
+                part_back(i).wait_recv()
+
+            def add(i, carry):
+                at = pl.ds(pl.multiple_of(i * 64, 64), 64)
+                acc[at, :] += part_in[at, :].astype(F32)
+                return carry
+
+            lax.fori_loop(0, acc.shape[0] // 64, add, 0)
+
+        @pl.when(helps)
+        def _():
+            for i in range(n_wide):
+                part_back(i).wait_send()
 
     lax.fori_loop(0, acc.shape[0] // 64, scaled, 0)
     last = pltpu.make_async_copy(kv, kv_out, out_sem.at[3])
@@ -288,15 +384,17 @@
         src = t // n_chunk
         k = t % n_chunk
 
-        @pl.when(jnp.logical_and(src <= z, z < n_line - 1))
+        @pl.when(jnp.logical_and(src <= z, goes_up(src, k)))
         def _():
             line_copy(src, k, True).wait_send()
 
-        @pl.when(jnp.logical_and(src >= z, z > 0))
+        @pl.when(jnp.logical_and(src >= z, goes_down(src, k)))
         def _():
             line_copy(src, k, False).wait_send()
 
-        pair_copy(src, k, core).wait_send()
+        @pl.when(jnp.logical_not(lent_out(z, src, k)))
+        def _():
+            pair_copy(src, k, core).wait_send()
         return carry
 
     lax.fori_loop(0, n_event, passed, 0)
@@ -312,10 +410,12 @@
     n_line = n_fsdp // 2
     chunk = min(128, rows)
     n_chunk = rows // chunk
+    first = n_chunk // 2 if n_line >= 4 else n_chunk
+    lent_rows = max(rows - first * chunk, 128)
     anywhere = pl.BlockSpec(memory_space=pl.ANY)
     dma = pltpu.SemaphoreType.DMA
     return pl.pallas_call(
-        functools.partial(kernel, n_rep, n_line, chunk, 32),
+        functools.partial(kernel, n_rep, n_line, chunk, 32, first),
         out_shape=(
             jax.ShapeDtypeStruct((count, cols), BF16),
             jax.ShapeDtypeStruct((1, rows, cols), BF16),
@@ -339,15 +439,19 @@
             pltpu.VMEM((n_rep, 8, part), F32),
             pltpu.VMEM((count, cols), F32),
             pltpu.VMEM((count, cols), BF16),
+            pltpu.VMEM((4, count, lent_rows), BF16),
+            pltpu.VMEM((count, cols), BF16),
+            pltpu.VMEM((count, cols), BF16),
             dma((4,)), dma((4,)),
             dma((n_rep - 1,)), dma((n_rep - 1,)),
             dma((n_rep - 1, n_chunk)), dma((n_rep - 1, n_chunk)),
             dma((n_rep - 1, n_chunk)), dma((n_rep - 1, n_chunk)),
             dma((n_line, n_chunk)), dma((n_line, n_chunk)), dma((n_line, n_chunk)),
             dma((n_line, n_chunk)), dma((n_line, n_chunk)),
+            dma((4,)), dma((4,)), dma((max(cols // 256, 1),)), dma((max(cols // 256, 1),)),
         ],
         compiler_params=pltpu.CompilerParams(
-            collective_id=0, has_side_effects=True, vmem_limit_bytes=56 * 2**20
+            collective_id=0, has_side_effects=True, vmem_limit_bytes=60 * 2**20
         ),
     )(step_counts, norm_gain.reshape(1, width), tokens, local_params, global_params, momentum)
 

time: 171 us -> 177 us (1.035)
  Pallas kernels: 161 us -> 167 us
    pallas_call x1, Pallas kernels: 161 us -> 167 us  [shards(): pl.pallas_call(functools.partial(kernel, n_rep, n_line, chunk, 32, first)...]
where the time goes in v2:
time: 177 us
  Pallas kernels  167 us (94%)
  local copies, waits for them, and re-layouts  8.3 us (5%)
    pallas_call x1, Pallas kernels, shards(): pl.pallas_call(functools.partial(kernel, n_rep, n_line, chunk, 32, first)...  167 us
    unnamed x10, local copies, waits for them, and re-layouts  6.95 us

profile of v2, /device:TPU:0, one launch (start us, length us, event | category | flops | bytes accessed | tf_op | source)
XLA Modules:
  0.0 176.7 jit_solution(2213503679088584737)
XLA Ops:
  1.3 1.4 reshape.11.gain
  2.6 167.1 %shard_map.93 = (bf16[512,1024]{1,0:T(8,128)(2,1)}, bf16[1,1024,1024]{2,1,0:T(8,128)(2,1)}, f32[1024,256]{1,0:T(8,128)}, f32[1024,256]{1,0:T(8,128)}) custom-call(s32[1]{0:T(128)S(6)} %copy.14.counts, bf16[1,8192]{1,0:T(2,128)(2,1)} %reshape.11.gain, bf16[512,8192]{1,0:T(8,128)(2,1)} %tok_hbm.1, bf16[1,1024,1024]{2,1,0:T(8,128)(2,1)} %loc_hbm.1, ...), custom_call_target="tpu_custom_call" | custom-call | tf_op jit(solution)/shard_map/pallas_call | solution.py:417
  169.7 0.0 copy-start
  169.7 2.4 %copy.15 = bf16[512,1024]{1,0:T(8,128)(2,1)} copy(bf16[512,1024]{1,0:T(8,128)(2,1)} %get-tuple-element.8) | data formatting | bytes 2097152
  172.1 0.0 copy-done
  172.1 0.0 copy-start.2
  172.1 1.3 copy.16
  173.4 0.6 copy-done.2
  174.1 0.0 copy-start.1
  174.1 1.0 copy.17
  175.1 0.6 copy-done.1
  175.7 1.0 copy.18
Async XLA Ops:
  169.7 2.4 %copy-start = (bf16[1,1024,1024]{2,1,0:T(8,128)(2,1)S(1)}, bf16[1,1024,1024]{2,1,0:T(8,128)(2,1)}, u32[]{:S(2)}) copy-start(bf16[1,1024,1024]{2,1,0:T(8,128)(2,1)} %get-tuple-element.9) | copy-start | bytes 6291460
  172.1 2.0 %copy-start.2 = (f32[1024,256]{1,0:T(8,128)S(1)}, f32[1024,256]{1,0:T(8,128)}, u32[]{:S(2)}) copy-start(f32[1024,256]{1,0:T(8,128)} %get-tuple-element.10) | copy-start | bytes 3145732
  174.1 1.6 copy-start.1

commit v3 on v2

--- a/solution.py
+++ b/solution.py
@@ -238,44 +238,6 @@
             for q in range(4):
                 lent_copy(q).start()
 
-    for k in range(n_chunk):
-        reduce_chunk(k)
-        if k + ahead < n_chunk:
-            send_parts(k + ahead)
-        if k >= 1:
-            mix_chunk(k - 1)
-    mix_chunk(n_chunk - 1)
-
-    if lend:
-        @pl.when(at_end)
-        def _():
-            for q in range(4):
-                lent_copy(q).wait_send()
-
-        @pl.when(z == 0)
-        def _():
-            for k in range(n_chunk):
-                line_copy(z, k, True).start()
-
-        @pl.when(z == n_line - 1)
-        def _():
-            for k in range(n_chunk):
-                line_copy(z, k, False).start()
-
-        @pl.when(jnp.logical_not(at_end))
-        def _():
-            norm()
-    else:
-        norm()
-
-    outs = [
-        pltpu.make_async_copy(glob, ng_out, out_sem.at[0]),
-        pltpu.make_async_copy(mom, nm_out, out_sem.at[1]),
-        pltpu.make_async_copy(w.at[f], nl_out.at[0], out_sem.at[2]),
-    ]
-    for one in outs:
-        one.start()
-
     def multiply(at, k):
         a = tok[:, pl.ds(pl.multiple_of(at * rows + k * chunk, chunk), chunk)]
 
@@ -326,8 +288,56 @@
 
     n_event = n_line * n_chunk
     n_tick = (n_line - 2) * n_chunk + n_chunk + n_line
-    receive(0)
-    lax.fori_loop(0, n_chunk, own, 0)
+    hold = 1
+    for k in range(n_chunk + 1):
+        if k < n_chunk:
+            reduce_chunk(k)
+            if k + ahead < n_chunk:
+                send_parts(k + ahead)
+        if k == 0:
+            if lend:
+                pl.when(jnp.logical_not(at_end))(norm)
+            else:
+                norm()
+        if k >= 1:
+            mix_chunk(k - 1)
+        if k >= 1 + hold:
+            t = k - 1 - hold
+            receive(t)
+            own(t, 0)
+            if t >= 1:
+                finish(t - 1)
+    caught = n_chunk - hold
+
+    if lend:
+        @pl.when(at_end)
+        def _():
+            for q in range(4):
+                lent_copy(q).wait_send()
+
+        @pl.when(z == 0)
+        def _():
+            for k in range(n_chunk):
+                line_copy(z, k, True).start()
+
+        @pl.when(z == n_line - 1)
+        def _():
+            for k in range(n_chunk):
+                line_copy(z, k, False).start()
+
+    outs = [
+        pltpu.make_async_copy(glob, ng_out, out_sem.at[0]),
+        pltpu.make_async_copy(mom, nm_out, out_sem.at[1]),
+        pltpu.make_async_copy(w.at[f], nl_out.at[0], out_sem.at[2]),
+    ]
+    for one in outs:
+        one.start()
+
+    receive(caught)
+    if caught >= 1:
+        finish(caught - 1)
+    for k in range(caught, n_chunk):
+        own(k, 0)
 
     def later(t, carry):
         receive(t)
@@ -338,7 +348,7 @@
                 help_end()
         return carry
 
-    lax.fori_loop(1, n_tick + 1, later, 0)
+    lax.fori_loop(caught + 1, n_tick + 1, later, 0)
 
     scale = (n_line * 2 * rows) ** (-0.5)
 
@@ -408,7 +418,7 @@
     _, rows, cols = local_params.shape
     part = cols // n_rep
     n_line = n_fsdp // 2
-    chunk = min(128, rows)
+    chunk = min(128, rows // 2)
     n_chunk = rows // chunk
     first = n_chunk // 2 if n_line >= 4 else n_chunk
     lent_rows = max(rows - first * chunk, 128)

time: 177 us -> 156 us (0.88)
  Pallas kernels: 167 us -> 146 us
    pallas_call x1, Pallas kernels: 167 us -> 146 us  [shards(): pl.pallas_call(functools.partial(kernel, n_rep, n_line, chunk, 32, first)...]
where the time goes in v3:
time: 156 us
  Pallas kernels  146 us (94%)
  local copies, waits for them, and re-layouts  8.3 us (5%)
    pallas_call x1, Pallas kernels, shards(): pl.pallas_call(functools.partial(kernel, n_rep, n_line, chunk, 32, first)...  146 us
    unnamed x10, local copies, waits for them, and re-layouts  6.95 us

profile of v3, /device:TPU:0, one launch (start us, length us, event | category | flops | bytes accessed | tf_op | source)
XLA Modules:
  0.0 156.0 jit_solution(1155182870792309183)
XLA Ops:
  1.3 1.4 reshape.11.gain
  2.6 146.4 %shard_map.93 = (bf16[512,1024]{1,0:T(8,128)(2,1)}, bf16[1,1024,1024]{2,1,0:T(8,128)(2,1)}, f32[1024,256]{1,0:T(8,128)}, f32[1024,256]{1,0:T(8,128)}) custom-call(s32[1]{0:T(128)S(6)} %copy.14.counts, bf16[1,8192]{1,0:T(2,128)(2,1)} %reshape.11.gain, bf16[512,8192]{1,0:T(8,128)(2,1)} %tok_hbm.1, bf16[1,1024,1024]{2,1,0:T(8,128)(2,1)} %loc_hbm.1, ...), custom_call_target="tpu_custom_call" | custom-call | tf_op jit(solution)/shard_map/pallas_call | solution.py:427
  149.0 0.0 copy-start
  149.0 2.4 %copy.15 = bf16[512,1024]{1,0:T(8,128)(2,1)} copy(bf16[512,1024]{1,0:T(8,128)(2,1)} %get-tuple-element.8) | data formatting | bytes 2097152
  151.4 0.0 copy-done
  151.4 0.0 copy-start.2
  151.4 1.3 copy.16
  152.8 0.6 copy-done.2
  153.4 0.0 copy-start.1
  153.4 1.0 copy.17
  154.4 0.6 copy-done.1
  155.0 1.0 copy.18
Async XLA Ops:
  149.0 2.4 %copy-start = (bf16[1,1024,1024]{2,1,0:T(8,128)(2,1)S(1)}, bf16[1,1024,1024]{2,1,0:T(8,128)(2,1)}, u32[]{:S(2)}) copy-start(bf16[1,1024,1024]{2,1,0:T(8,128)(2,1)} %get-tuple-element.9) | copy-start | bytes 6291460
  151.4 2.0 %copy-start.2 = (f32[1024,256]{1,0:T(8,128)S(1)}, f32[1024,256]{1,0:T(8,128)}, u32[]{:S(2)}) copy-start(f32[1024,256]{1,0:T(8,128)} %get-tuple-element.10) | copy-start | bytes 3145732
  153.4 1.6 %copy-start.1 = (f32[1024,256]{1,0:T(8,128)S(1)}, f32[1024,256]{1,0:T(8,128)}, u32[]{:S(2)}) copy-start(f32[1024,256]{1,0:T(8,128)} %get-tuple-element.11) | copy-start | bytes 3145732

commit v4 on v3

--- a/solution.py
+++ b/solution.py
@@ -215,7 +215,7 @@
             return carry
 
         lax.fori_loop(0, chunk // step, some, 0)
-        inner = jnp.logical_not(at_end) if lend else True
+        inner = jnp.logical_not(at_end) if lend and k < n_chunk // 2 else True
         pass_on(z, k, inner, inner)
 
     def norm():
@@ -300,6 +300,17 @@
             else:
                 norm()
         if k >= 1:
+            if lend and k - 1 == n_chunk // 2:
+                @pl.when(z == 0)
+                def _():
+                    for held in range(n_chunk // 2):
+                        line_copy(z, held, True).start()
+
+                @pl.when(z == n_line - 1)
+                def _():
+                    for held in range(n_chunk // 2):
+                        line_copy(z, held, False).start()
+
             mix_chunk(k - 1)
         if k >= 1 + hold:
             t = k - 1 - hold
@@ -309,22 +320,6 @@
                 finish(t - 1)
     caught = n_chunk - hold
 
-    if lend:
-        @pl.when(at_end)
-        def _():
-            for q in range(4):
-                lent_copy(q).wait_send()
-
-        @pl.when(z == 0)
-        def _():
-            for k in range(n_chunk):
-                line_copy(z, k, True).start()
-
-        @pl.when(z == n_line - 1)
-        def _():
-            for k in range(n_chunk):
-                line_copy(z, k, False).start()
-
     outs = [
         pltpu.make_async_copy(glob, ng_out, out_sem.at[0]),
         pltpu.make_async_copy(mom, nm_out, out_sem.at[1]),
@@ -360,6 +355,8 @@
     if lend:
         @pl.when(at_end)
         def _():
+            for q in range(4):
+                lent_copy(q).wait_send()
             for i in range(n_wide):
                 part_back(i).wait_recv()
 

time: 156 us -> 156 us (level)
  no operation moved by 1% of the time
where the time goes in v4:
time: 156 us
  Pallas kernels  146 us (94%)
  local copies, waits for them, and re-layouts  8.3 us (5%)
    pallas_call x1, Pallas kernels, shards(): pl.pallas_call(functools.partial(kernel, n_rep, n_line, chunk, 32, first)...  146 us
    unnamed x10, local copies, waits for them, and re-layouts  6.95 us

profile of v4, /device:TPU:0, one launch (start us, length us, event | category | flops | bytes accessed | tf_op | source)
XLA Modules:
  0.0 156.0 jit_solution(15895363040141019381)
XLA Ops:
  1.3 1.4 reshape.11.gain
  2.6 146.4 %shard_map.93 = (bf16[512,1024]{1,0:T(8,128)(2,1)}, bf16[1,1024,1024]{2,1,0:T(8,128)(2,1)}, f32[1024,256]{1,0:T(8,128)}, f32[1024,256]{1,0:T(8,128)}) custom-call(s32[1]{0:T(128)S(6)} %copy.14.counts, bf16[1,8192]{1,0:T(2,128)(2,1)} %reshape.11.gain, bf16[512,8192]{1,0:T(8,128)(2,1)} %tok_hbm.1, bf16[1,1024,1024]{2,1,0:T(8,128)(2,1)} %loc_hbm.1, ...), custom_call_target="tpu_custom_call" | custom-call | tf_op jit(solution)/shard_map/pallas_call | solution.py:424
  149.0 0.0 copy-start
  149.0 2.4 %copy.15 = bf16[512,1024]{1,0:T(8,128)(2,1)} copy(bf16[512,1024]{1,0:T(8,128)(2,1)} %get-tuple-element.8) | data formatting | bytes 2097152
  151.4 0.0 copy-done
  151.4 0.0 copy-start.2
  151.4 1.3 copy.16
  152.8 0.6 copy-done.2
  153.4 0.0 copy-start.1
  153.4 1.0 copy.17
  154.4 0.6 copy-done.1
  155.0 1.0 copy.18
Async XLA Ops:
  149.0 2.4 %copy-start = (bf16[1,1024,1024]{2,1,0:T(8,128)(2,1)S(1)}, bf16[1,1024,1024]{2,1,0:T(8,128)(2,1)}, u32[]{:S(2)}) copy-start(bf16[1,1024,1024]{2,1,0:T(8,128)(2,1)} %get-tuple-element.9) | copy-start | bytes 6291460
  151.4 2.0 %copy-start.2 = (f32[1024,256]{1,0:T(8,128)S(1)}, f32[1024,256]{1,0:T(8,128)}, u32[]{:S(2)}) copy-start(f32[1024,256]{1,0:T(8,128)} %get-tuple-element.10) | copy-start | bytes 3145732
  153.4 1.6 %copy-start.1 = (f32[1024,256]{1,0:T(8,128)S(1)}, f32[1024,256]{1,0:T(8,128)}, u32[]{:S(2)}) copy-start(f32[1024,256]{1,0:T(8,128)} %get-tuple-element.11) | copy-start | bytes 3145732
